TPU v7x, 512 devices: a whole 4x4x16 slice. The times are simulated.
512 devices in a mesh: blk: 128 (over y_hi, x, z), grp: 4 (over y_lo, core).
Axes of the slice: x: 4, y: 4 (y_hi: 2, y_lo: 2; y = y_hi * 2 + y_lo), z: 16, core: 2. Of those that a mesh axis runs over, the one named last changes fastest.
Arguments:
- orbitals: bfloat16 [3072, 2, 8, 128], P(('blk', 'grp')), may hold values from -2.390625 to 2.390625
- screen: bfloat16 [128, 24, 2, 128, 128], P('blk', 'grp'), may hold values from -0.375 to 0.375
- slot_of_q: int32 [3, 24], replicated, may hold values from 0 to 23, as said below
Outputs:
- lower: bfloat16 [128, 3, 2, 384, 384], P('blk', None, None, None, 'grp')
- upper: bfloat16 [128, 2, 2, 384, 384], P('blk', None, None, 'grp')
Inputs may be any that keep to these rules, and one draw needn't show every extreme that they name: Each row of slot_of_q is a permutation of 0 to 23.
All inputs are finite; a program needn't handle non-finite values.
Results may differ from a plain program's by a relative error of at most 0.0064.
Values may be sent and summed in bfloat16 or wider, within the bound.
A program may use at most 64 MiB of HBM per device.

v0:
```python
import jax
import jax.numpy as jnp
from jax import lax
from jax.sharding import PartitionSpec as P

STEPS = 3


def shifted(value, axis, steps):
    count = lax.axis_size(axis)
    pairs = [(source, (source + steps) % count) for source in range(count)]
    return lax.ppermute(value, axis, pairs)


def spread(array, axis, root):
    mine = lax.axis_index(axis) == root
    return lax.psum(jnp.where(mine, array, jnp.zeros_like(array)), axis)


def group_kernel(rolled_rows, partner_rows, screen_by_q):
    half_bands = rolled_rows.shape[3] // 2
    group_count = rolled_rows.shape[0]
    count_q = rolled_rows.shape[1]
    points = rolled_rows.shape[4]

    def densities(first_band, last_band):
        first_real = rolled_rows[:, :, 0, first_band:last_band, None, :].astype(jnp.float32)
        first_imag = rolled_rows[:, :, 1, first_band:last_band, None, :].astype(jnp.float32)
        second_real = partner_rows[:, None, 0, None, first_band:last_band, :].astype(jnp.float32)
        second_imag = partner_rows[:, None, 1, None, first_band:last_band, :].astype(jnp.float32)
        real_part = first_real * second_real + first_imag * second_imag
        imag_part = first_real * second_imag - first_imag * second_real
        shape_out = (group_count, count_q, half_bands * half_bands, points)
        return (
            real_part.reshape(shape_out).astype(jnp.bfloat16),
            imag_part.reshape(shape_out).astype(jnp.bfloat16),
        )

    cond_real, cond_imag = densities(half_bands, 2 * half_bands)
    val_real, val_imag = densities(0, half_bands)
    screen_real = screen_by_q[:, 0]
    screen_imag = screen_by_q[:, 1]

    def apply_screen(left, right):
        return jnp.einsum("gqam,qmn->gqan", left, right, preferred_element_type=jnp.float32)

    def close_pairs(left, right):
        return jnp.einsum("gqan,gqbn->gqab", left, right, preferred_element_type=jnp.float32)

    mixed_real = (
        apply_screen(cond_real, screen_real) - apply_screen(cond_imag, screen_imag)
    ).astype(jnp.bfloat16)
    mixed_imag = (
        apply_screen(cond_real, screen_imag) + apply_screen(cond_imag, screen_real)
    ).astype(jnp.bfloat16)
    kernel_real = close_pairs(mixed_real, val_real) + close_pairs(mixed_imag, val_imag)
    kernel_imag = close_pairs(mixed_imag, val_real) - close_pairs(mixed_real, val_imag)
    stacked = jnp.stack([kernel_real, kernel_imag], axis=1)
    stacked = stacked.reshape(
        group_count, 2, count_q, half_bands, half_bands, half_bands, half_bands
    )
    stacked = stacked.transpose(0, 1, 2, 3, 5, 4, 6)
    return stacked.reshape(
        group_count, 2, count_q, half_bands * half_bands, half_bands * half_bands
    ).astype(jnp.bfloat16)


def take_rows(block, order):
    return jnp.take(block, order, axis=1)


def body(orbitals, screen, slot_of_q):
    sub_points = orbitals.shape[0]
    group_id = lax.axis_index("grp")
    left_rows = lax.all_gather(orbitals, "grp", axis=0, tiled=True)
    block_points = left_rows.shape[0]
    pair_count = (left_rows.shape[2] // 2) ** 2
    ramp = jnp.arange(block_points, dtype=jnp.int32)
    right_rows = orbitals
    lower_blocks = []
    for cycle_step in range(STEPS):
        if cycle_step > 0:
            right_rows = shifted(right_rows, "blk", 1)
        screen_piece = spread(screen[0], "blk", cycle_step)
        screen_row = lax.all_gather(screen_piece, "grp", axis=0, tiled=True)
        screen_by_q = jnp.take(screen_row, slot_of_q[cycle_step], axis=0)
        local_points = jnp.arange(sub_points, dtype=jnp.int32)
        global_points = group_id * sub_points + local_points
        forward = jnp.mod(global_points[:, None] + ramp[None, :], block_points)
        rolled_rows = jnp.take(left_rows, forward, axis=0)
        kernel_q = group_kernel(rolled_rows, right_rows, screen_by_q)
        backward = jnp.mod(ramp[None, :] - global_points[:, None], block_points)
        gathered_columns = jax.vmap(take_rows)(kernel_q, backward)
        finished = gathered_columns.transpose(1, 2, 3, 0, 4).reshape(
            2, block_points * pair_count, sub_points * pair_count
        )
        lower_blocks.append(finished)
    mirrored = [
        jnp.stack([lower_blocks[offset][0].T, -lower_blocks[offset][1].T])
        for offset in range(STEPS)
    ]
    upper_blocks = [shifted(mirrored[offset], "blk", -offset) for offset in range(1, STEPS)]
    return (jnp.stack(lower_blocks)[None], jnp.stack(upper_blocks)[None])


def solution(mesh):
    in_specs = (P(("blk", "grp"), None, None, None), P("blk", "grp", None, None, None), P())
    out_specs = (P("blk", None, None, None, "grp"), P("blk", None, None, "grp", None))
    return jax.shard_map(body, mesh=mesh, in_specs=in_specs, out_specs=out_specs, check_vma=False)
```

profile of v0, /device:TPU:1, one launch (start us, length us, event | category | flops | bytes accessed | tf_op | source)
XLA Modules:
  0.0 1498.7 jit_solution(16042518404260418535)
XLA Ops:
  7.2 2.0 select_bitcast_fusion.5
  9.3 1241.2 %all-reduce.3.cloned.1.call-done = (bf16[6,2,128,128]{3,2,1,0:T(8,128)(2,1)}, bf16[6,2,128,128]{3,2,1,0:T(8,128)(2,1)}, bf16[6,2,128,128]{3,2,1,0:T(8,128)(2,1)}) async-done(((bf16[6,2,128,128]{3,2,1,0:T(8,128)(2,1)}, bf16[6,2,128,128]{3,2,1,0:T(8,128)(2,1)}, bf16[6,2,128,128]{3,2,1,0:T(8,128)(2,1)}), (bf16[6,2,128,128]{3,2,1,0:T(8,128)(2,1)}, bf16[6,2,128,128]{3,2,1,0:T(8,128)(2,1)}, ...) | async-done | bytes 1179664 | tf_op jit(solution)/shard_map/psum | solution.py:17
  1250.6 0.7 all-gather.4.cloned.1.call-update
  1251.3 1.9 collective-permute-start
  1253.4 64.4 %all_gather.13 = bf16[24,2,8,128]{3,2,1,0:T(8,128)(2,1)S(1)} all-gather(bf16[6,2,8,128]{3,2,1,0:T(8,128)(2,1)S(1)} %copy-done.23), channel_id=1, replica_groups=mesh['blk'=128,'grp'=4] {'grp'}, dimensions={0}, use_global_device_ids=true | all-gather | bytes 122880 | tf_op jit(solution)/shard_map/all_gather | solution.py:75
  1317.8 0.7 gather_fusion.1
  1319.6 1.9 collective-permute-start.1
  1321.5 8.7 collective-permute-done.1
  1331.0 2.4 subtract_convert_fusion.5
  1334.0 2.5 subtract_convert_fusion.4
  1336.4 3.4 gather_fusion.5
  1339.8 30.4 %all-gather.4.cloned.1.call-done = bf16[24,2,128,128]{3,2,1,0:T(8,128)(2,1)} async-done(((bf16[6,2,128,128]{3,2,1,0:T(8,128)(2,1)}), bf16[24,2,128,128]{3,2,1,0:T(8,128)(2,1)}) %all-gather.4.cloned.1.call-update) | async-done | bytes 1572880 | tf_op jit(solution)/shard_map/all_gather | solution.py:85
  1370.2 2.3 gather_fusion
  1372.6 0.8 copy-done.3
  1373.5 1.4 fusion.19
  1374.9 1.4 fusion.18
  1376.3 29.6 %all-gather.6.cloned.1.call-done = bf16[24,2,128,128]{3,2,1,0:T(8,128)(2,1)} async-done(((bf16[6,2,128,128]{3,2,1,0:T(8,128)(2,1)}), bf16[24,2,128,128]{3,2,1,0:T(8,128)(2,1)}) %all-gather.6.cloned.1.call-update) | async-done | bytes 1572880 | tf_op jit(solution)/shard_map/all_gather | solution.py:85
  1405.8 3.3 gather_fusion.3
  1409.2 1.8 copy_select_fusion
  1411.7 0.7 copy-done.1
  1413.1 0.7 copy-done.10
  1414.6 0.9 copy-done.15
  1415.9 0.9 copy-done.9
  1417.5 0.7 copy-done.7
  1419.0 0.7 copy-done.12
  1420.1 1.5 fusion.40
  1421.6 1.3 fusion.1
  1422.9 2.3 copy.138
  1425.2 2.5 fusion
  1427.7 1.6 copy.135
  1429.3 0.6 maximum_bitcast_fusion
  1430.0 1.3 copy.139
  1431.2 2.0 copy.140
  1433.3 2.9 gather_fusion.2
  1436.1 3.3 copy.177
  1439.9 1.5 fusion.28
  1441.8 1.2 copy.161
  1443.1 1.7 fusion.4
  1444.8 0.5 copy.158
  1445.8 0.6 maximum_bitcast_fusion.2
  1446.8 1.1 copy.163
  1447.9 1.8 gather_fusion.6
  1449.7 1.9 copy.165
  1452.5 0.6 copy-done.4
  1453.5 1.2 copy.149
  1455.3 0.5 copy.146
  1456.2 0.6 maximum_bitcast_fusion.1
  1457.2 1.3 copy.151
  1458.6 1.8 gather_fusion.4
  1460.4 1.1 copy.153
  1461.8 0.5 copy.167
  1463.6 10.0 collective-permute-start.2
  1473.6 0.8 fusion.61
  1475.3 1.4 copy.170
  1477.2 3.8 collective-permute-start.3
  1481.0 1.1 select_bitcast_fusion
  1482.1 1.0 copy.154
  1483.1 1.7 copy.166
  1484.8 2.0 copy.142
  1486.9 0.8 stack_reshape.9
  1487.7 0.8 stack_reshape.10
  1488.9 0.8 stack_reshape.11
  1489.7 0.8 maximum_bitcast_fusion.3
  1490.5 1.7 maximum_bitcast_fusion.4
  (117 shorter events, 14.7 us)
Async XLA Ops:
  7.2 1243.3 %all-reduce.3.cloned.1.call-start = ((), (), s32[]{:S(2)}) async-start(), calls=%async_computation.3 | async-start | bytes 2359296 | tf_op jit(solution)/shard_map/psum | solution.py:17
  9.3 1242.1 %copy-start.23 = (bf16[6,2,8,128]{3,2,1,0:T(8,128)(2,1)S(1)}, bf16[6,2,8,128]{3,2,1,0:T(8,128)(2,1)}, u32[]{:S(2)}) copy-start(bf16[6,2,8,128]{3,2,1,0:T(8,128)(2,1)} %param.9) | copy-start | bytes 73732
  9.3 1309.4 %copy-start.24 = (s32[3,24]{1,0:T(4,128)S(1)}, s32[3,24]{1,0:T(4,128)}, u32[]{:S(2)}) copy-start(s32[3,24]{1,0:T(4,128)} %param.11) | copy-start | bytes 868
  9.3 1327.1 %all-gather.8.cloned.1.call-start = ((), (), s32[]{:S(2)}) async-start(), calls=%async_computation.2 | async-start | bytes 1966080 | tf_op jit(solution)/shard_map/all_gather | solution.py:85
  1250.5 119.6 %all-gather.4.cloned.1.call-start = ((), (), s32[]{:S(2)}) async-start(), calls=%async_computation | async-start | bytes 1966080 | tf_op jit(solution)/shard_map/all_gather | solution.py:85
  1251.3 154.6 %all-gather.6.cloned.1.call-start = ((), (), s32[]{:S(2)}) async-start(), calls=%async_computation.1 | async-start | bytes 1966080 | tf_op jit(solution)/shard_map/all_gather | solution.py:85
  1251.3 68.2 %collective-permute-start = (bf16[6,2,8,128]{3,2,1,0:T(8,128)(2,1)S(1)}, bf16[6,2,8,128]{3,2,1,0:T(8,128)(2,1)S(1)}, u32[]{:S(2)}, u32[]{:S(2)}) collective-permute-start(bf16[6,2,8,128]{3,2,1,0:T(8,128)(2,1)S(1)} %copy-done.23), channel_id=1, source_target_pairs={{0,4},{4,8},{8,12},{12,16},{16,20},{20,24},{24,28},{28,32},{32,36}... | collective-permute-start | bytes 73736 | tf_op jit(solution)/shard_map/ppermute | solution.py:12
  1319.6 10.7 collective-permute-start.1
  1372.4 1.1 copy-start.3
  1376.3 32.9 %copy-start = (bf16[24,2,128,128]{3,2,1,0:T(8,128)(2,1)S(1)}, bf16[24,2,128,128]{3,2,1,0:T(8,128)(2,1)}, u32[]{:S(2)}) copy-start(bf16[24,2,128,128]{3,2,1,0:T(8,128)(2,1)} %gather_fusion.5) | copy-start | bytes 4718596
  1409.2 1.8 copy-start.2
  1411.4 1.1 copy-start.1
  1412.8 1.1 copy-start.10
  1412.8 1.4 copy-start.16
  1414.2 1.3 copy-start.15
  1415.5 3.5 copy-start.13
  1415.5 1.3 copy-start.9
  1417.2 1.1 copy-start.7
  1418.6 1.1 copy-start.12
  1420.1 1.5 copy-start.11
  1422.9 2.3 copy-start.14
  1427.7 1.6 copy-start.20
  1436.1 3.3 copy-start.8
  1439.8 1.5 copy-start.6
  1444.8 1.0 copy-start.21
  1449.7 1.9 copy-start.5
  1452.0 1.1 copy-start.4
  1455.2 1.0 copy-start.22
  1460.4 1.2 copy-start.19
  1463.6 26.9 %collective-permute-start.2 = (bf16[2,96,384]{2,1,0:T(8,128)(2,1)S(1)}, bf16[2,96,384]{2,1,0:T(8,128)(2,1)}, u32[]{:S(2)}, u32[]{:S(2)}) collective-permute-start(bf16[2,96,384]{2,1,0:T(8,128)(2,1)S(1)} %pad_maximum_fusion), channel_id=1, source_target_pairs={{0,508},{4,0},{8,4},{12,8},{16,12},{20,16},{24,20},{28,24},{32,28}... | collective-permute-start | bytes 442376 | tf_op jit(solution)/shard_map/ppermute | solution.py:12
  1474.9 6.1 copy-start.18
  1477.2 13.4 collective-permute-start.3
  1487.6 1.3 copy-start.17
Sparse Core Ops, SparseCore 0:
  11.7 1238.7 all-reduce.2
  1252.8 82.2 all-gather.7
  1337.4 32.6 all-gather.3
  1372.3 33.4 all-gather.5
where the time goes:
time: 1500 us
  waiting for transfers between devices  1310 us (87%)
  blocking collectives  64.4 us (4%)
  local copies, waits for them, and re-layouts  57.1 us (4%)
  matrix products  18 us (1%)
  starting transfers between devices  17.8 us (1%)
  other arithmetic  16.4 us (1%)
    psum x1, waiting for transfers between devices, spread(): return lax.psum(jnp.where(mine, array, jnp.zeros_like(array)), axis)  1240 us
    all_gather x1, blocking collectives, body(): left_rows = lax.all_gather(orbitals, 'grp', axis=0, tiled=True)  64.4 us
    all_gather x3, waiting for transfers between devices, body(): screen_row = lax.all_gather(screen_piece, 'grp', axis=0, tiled=True)  59.9 us
  transfers between devices with their start and end apart: 8, of which 4 were waited for; matrix products, arithmetic and copies ran while one was open for 2% of the time, Pallas kernels for 0%

commit v1 on v0

v1 whole, which is shorter than its diff:
```python
import functools
import jax
import jax.numpy as jnp
from jax import lax
from jax.experimental import pallas as pl
from jax.experimental.pallas import tpu as pltpu
from jax.sharding import PartitionSpec as P

BF = jnp.bfloat16
F32 = jnp.float32


def select_matrix(tile):
    r = lax.broadcasted_iota(jnp.int32, (256, 128), 0)
    col = lax.broadcasted_iota(jnp.int32, (256, 128), 1)
    band = (r % 4) if tile else ((r // 4) % 4)
    return (col == (r // 16) * 8 + 4 + band).astype(F32).astype(BF)


def expand_rows(x, dst, stage, sel):
    x2 = x.reshape(384, 128)
    for i in range(3):
        dst[pl.ds(i * 256, 256), :] = jnp.dot(sel, x2[i * 128:(i + 1) * 128], preferred_element_type=F32)
    stage[...] = x2.astype(F32)


def valence(stage, dst):
    for p in range(2):
        for v in range(4):
            dst[p * 4 + v] = stage[pl.ds(p * 8 + v, 24, stride=16), :]


def expand_cols(x, dst, pt, sel):
    x2 = x.reshape(96, 128)
    dst[...] = jnp.dot(sel[:192, :96], x2, preferred_element_type=F32)
    n = lax.broadcasted_iota(jnp.int32, (8, 128), 0)
    l = lax.broadcasted_iota(jnp.int32, (8, 128), 1)
    g = (n == l % 4).astype(F32)
    dn = (((0,), (0,)), ((), ()))
    for j in range(6):
        a = lax.dot_general(x[j, 0].astype(F32), g, dn, preferred_element_type=F32).astype(BF)
        b = lax.dot_general(x[j, 1].astype(F32), g, dn, preferred_element_type=F32).astype(BF)
        pt[j, 0:128, 0:128] = a
        pt[j, 0:128, 128:256] = -b
        pt[j, 128:256, 0:128] = b
        pt[j, 128:256, 128:256] = a


def mix(load_w, slot_ref, s, g6, jobs):
    def step(q, carry):
        wr, wi = load_w(slot_ref[s, q])
        wc = jnp.concatenate([jnp.concatenate([wr, wi], 1), jnp.concatenate([-wi, wr], 1)], 0)
        rows = []
        for urep, utile, _, _ in jobs:
            for j in range(6):
                k = lax.rem(g6 + j + q, 24)
                at = pl.multiple_of(k * 32, 32)
                ar = urep[pl.ds(at, 16), :]
                ai = urep[pl.ds(at + 16, 16), :]
                br = utile[j * 32:j * 32 + 16, :]
                bi = utile[j * 32 + 16:j * 32 + 32, :]
                rows.append(jnp.concatenate([(ar * br + ai * bi).astype(BF), (ar * bi - ai * br).astype(BF)], 1))
        y = jnp.dot(jnp.concatenate(rows, 0), wc, preferred_element_type=F32)
        for n, (_, _, yr, yi) in enumerate(jobs):
            for j in range(6):
                k = lax.rem(g6 + j + q, 24)
                r0 = (n * 6 + j) * 16
                yr[pl.ds(j * 384 + k, 16, stride=24), :] = y[r0:r0 + 16, 0:128]
                yi[pl.ds(j * 384 + k, 16, stride=24), :] = y[r0:r0 + 16, 128:256]
        return carry
    lax.fori_loop(0, 24, step, 0, unroll=8)


def close(yr, yi, uv, pt, acc, tr, ti):
    lane = lax.broadcasted_iota(jnp.int32, (256, 256), 1) % 128 // 4

    def step(j, carry):
        ur = uv[0:4]
        ui = uv[4:8]
        p = pt[j]
        weights = jnp.concatenate([jnp.where(lane == j * 4 + c2, p, jnp.zeros_like(p)) for c2 in range(4)], 0)
        blocks = []
        for c in range(4):
            parts = []
            for c2 in range(4):
                at = pl.multiple_of(j * 384 + (c * 4 + c2) * 24, 8)
                a = yr[pl.ds(at, 24), :][None]
                b = yi[pl.ds(at, 24), :][None]
                parts.append((a * ur - b * ui).reshape(96, 128).astype(BF))
                parts.append((a * ui + b * ur).reshape(96, 128).astype(BF))
            blocks.append(jnp.concatenate(parts, 1))
        d = jnp.dot(jnp.concatenate(blocks, 0), weights, preferred_element_type=F32)

        acc[...] += d
        return carry
    acc[...] = jnp.zeros_like(acc)
    lax.fori_loop(0, 6, step, 0, unroll=6)
    for cv in range(16):
        tr[pl.ds(cv, 24, stride=16), :] = acc[cv * 24:cv * 24 + 24, 0:128]
        ti[pl.ds(cv, 24, stride=16), :] = acc[cv * 24:cv * 24 + 24, 128:256]


def emit_lower(tr, ti, out, s):
    out[0, s, 0] = tr[:, 0:96].astype(BF)
    out[0, s, 1] = ti[:, 0:96].astype(BF)


def emit_upper(tr, ti, out, t):
    out[0, t, 0] = tr[...].T[0:96, :].astype(BF)
    out[0, t, 1] = (-ti[...]).T[0:96, :].astype(BF)


def scratch():
    return dict(
        urep=[pltpu.VMEM((768, 128), F32)] * 3,
        uv=[pltpu.VMEM((8, 24, 128), F32)] * 3,
        utile=[pltpu.VMEM((192, 128), F32)] * 3,
        pt=[pltpu.VMEM((6, 256, 256), BF)] * 3,
        stage=pltpu.VMEM((384, 128), F32),
        yr=[pltpu.VMEM((2304, 128), F32)] * 2,
        yi=[pltpu.VMEM((2304, 128), F32)] * 2,
        acc=pltpu.VMEM((384, 256), F32),
        tr=pltpu.VMEM((384, 128), F32),
        ti=pltpu.VMEM((384, 128), F32),
    )


MESH = pl.DeviceIdType.MESH


def place():
    b = lax.axis_index("blk")
    g = lax.axis_index("grp")
    return (b // 16) % 4, (b // 64) * 2 + g // 2, b % 16, g % 2


def at_chip(x, y, z, c):
    x, y, z = lax.rem(x, 4), lax.rem(y, 4), lax.rem(z, 16)
    return (y // 2) * 64 + x * 16 + z, (y % 2) * 2 + c


class Exchange:
    def __init__(self, screen, orb, wbuf, rows, subs, sems):
        self.screen, self.orb, self.wbuf, self.rows, self.subs = screen, orb, wbuf, rows, subs
        self.sems = sems
        self.x, self.y, self.z, self.c = place()
        self.b, self.g = lax.axis_index("blk"), lax.axis_index("grp")
        self.h = jnp.where((self.y == 1) | (self.y == 2), 1, 0)
        self.yh = self.y // 2
        self.source = (self.x == 0) & (self.y < 2) & (self.z < 3)
        self.pending = []

    def row(self, off):
        return lax.rem(self.b + off + 128, 128)

    def barrier(self):
        bar = pltpu.get_barrier_semaphore()
        x, y, z, c = self.x, self.y, self.z, self.c
        near = [at_chip(x + d, y, z, c) for d in (1, 2, 3)] + [at_chip(x, y + d, z, c) for d in (1, 2, 3)]
        near += [at_chip(x, y, z + d, c) for d in (1, 2, 3, 13, 14, 15)]
        near += [(self.b, lax.rem(self.g + d, 4)) for d in (1, 2, 3)]
        near += [(self.row(d), self.g) for d in (1, 2, -1, -2)]
        for d in near:
            pl.semaphore_signal(bar, inc=1, device_id=d, device_id_type=MESH)

        @pl.when(self.source)
        def _():
            for xx in range(4):
                for yh in range(2):
                    if xx or yh:
                        pl.semaphore_signal(bar, inc=1, device_id=self.target(xx, yh), device_id_type=MESH)

        @pl.when((z < 3) & jnp.logical_not(self.source))
        def _():
            pl.semaphore_signal(bar, inc=1, device_id=at_chip(0, self.h, z, c), device_id_type=MESH)
        extra = jnp.where(self.source, 7, jnp.where(z < 3, 1, 0))
        pl.semaphore_wait(bar, len(near) + extra)

    def target(self, xx, yh):
        return at_chip(xx, self.y if yh == 0 else 3 - self.y, self.z, self.c)

    def remote(self, src, dst, send, recv, to):
        return pltpu.make_async_remote_copy(src_ref=src, dst_ref=dst, send_sem=send, recv_sem=recv, device_id=to, device_id_type=MESH)

    def launch(self, cp, cond=None):
        if cond is None:
            cp.start()
        else:
            pl.when(cond)(lambda: cp.start())
        self.pending.append((cp, cond))

    def unit(self, half, x):
        return pl.ds(half * 12 + x * 3, 3)

    def own(self, s, half):
        return self.wbuf.at[s, self.h, self.c, self.yh, self.unit(half, self.x)]

    def scatter(self):
        sm, z = self.sems, self.z

        @pl.when(self.source)
        def _():
            for half in range(2):
                for xx, yh in ((2, 1), (1, 1), (3, 1), (2, 0), (1, 0), (3, 0), (0, 1)):
                    self.remote(self.screen.at[yh, self.unit(half, xx)], self.wbuf.at[z, self.h, self.c, yh, self.unit(half, xx)],
                                sm["scat"].at[half, xx, yh], sm["own"].at[z, half], self.target(xx, yh)).start()
                pltpu.make_async_copy(self.screen.at[0, self.unit(half, 0)], self.wbuf.at[z, self.h, self.c, 0, self.unit(half, 0)],
                                      sm["own"].at[z, half]).start()

    def drain_scatter(self):
        @pl.when(self.source)
        def _():
            for half in range(2):
                for xx, yh in ((2, 1), (1, 1), (3, 1), (2, 0), (1, 0), (3, 0), (0, 1)):
                    self.remote(self.screen.at[yh, self.unit(half, xx)], self.wbuf.at[self.z, self.h, self.c, yh, self.unit(half, xx)],
                                self.sems["scat"].at[half, xx, yh], self.sems["own"].at[self.z, half], self.target(xx, yh)).wait_send()

    def orbitals_out(self):
        sm, g = self.sems, self.g
        self.o_in = []
        local = [pltpu.make_async_copy(self.orb, self.rows.at[0, pl.ds(g * 6, 6)], sm["oloc"].at[0]),
                 pltpu.make_async_copy(self.orb, self.subs.at[0], sm["oloc"].at[1])]
        for cp in local:
            cp.start()
        self.o_local = local
        for n, (off, dst) in enumerate(((-1, self.rows.at[1, pl.ds(g * 6, 6)]), (-2, self.rows.at[2, pl.ds(g * 6, 6)]),
                                        (1, self.subs.at[1]), (2, self.subs.at[2]))):
            cp = self.remote(self.orb, dst, sm["os"].at[n], sm["or"].at[n], (self.row(off), g))
            self.launch(cp)
            self.o_in.append(cp)
        self.group_out(0, self.orb, 4)

    def group_out(self, r, src, base):
        for d in (1, 2, 3):
            n = base + d - 1
            cp = self.remote(src, self.rows.at[r, pl.ds(self.g * 6, 6)], self.sems["os"].at[n], self.sems["or"].at[n],
                             (self.b, lax.rem(self.g + d, 4)))
            self.launch(cp)
            back = lax.rem(self.g + 4 - d, 4)
            self.o_in.append(self.remote(src, self.rows.at[r, pl.ds(back * 6, 6)], self.sems["os"].at[n], self.sems["or"].at[n],
                                         (self.b, lax.rem(self.g + d, 4))))

    def orbitals_on(self):
        for r in (1, 2):
            self.o_in[r - 1].wait_recv()
            self.group_out(r, self.rows.at[r, pl.ds(self.g * 6, 6)], 4 + 3 * r)

    def orbitals_done(self):
        for cp in self.o_local:
            cp.wait()
        for cp in self.o_in[2:]:
            cp.wait_recv()

    def first(self, s):
        sm, x, y, z, c = self.sems, self.x, self.y, self.z, self.c
        dz = lax.rem(z + 16 - s, 16)
        hub = (dz == 0) | (dz == 3) | (dz == 6) | (dz == 10) | (dz == 13)
        hops = ((3, (dz == 0) | (dz == 3)), (13, (dz == 0) | (dz == 13)), (2, dz == 6), (1, hub), (15, hub))
        for half in range(2):
            mine = self.own(s, half)
            self.remote(mine, mine, sm["zs"].at[s, 0, half], sm["own"].at[s, half], (self.b, self.g)).wait_recv()
            for n, (off, cond) in enumerate(hops):
                self.launch(self.remote(mine, mine, sm["zs"].at[s, n, half], sm["own"].at[s, half], at_chip(x, y, z + off, c)), cond)
        for half in range(2):
            mine = self.own(s, half)
            for d in (2, 1, 3):
                to = at_chip(x + d, y, z, c) if half == 0 else at_chip(x, y + d, z, c)
                self.launch(self.remote(mine, mine, sm["p1s"].at[s, half, d - 1], sm["p1r"].at[s, half, d - 1], to))

    def split(self, y):
        return jnp.where((y == 1) | (y == 2), 1, 0), y // 2

    def second(self, s):
        sm, x, y, z, c = self.sems, self.x, self.y, self.z, self.c
        for half in range(2):
            for d in (1, 3, 2):
                if half == 0:
                    there = self.wbuf.at[s, self.h, c, self.yh, self.unit(0, lax.rem(x + 4 - d, 4))]
                else:
                    hh, yy = self.split(lax.rem(y + 4 - d, 4))
                    there = self.wbuf.at[s, hh, c, yy, self.unit(1, x)]
                self.remote(there, there, sm["p1s"].at[s, half, d - 1], sm["p1r"].at[s, half, d - 1], (self.b, self.g)).wait_recv()
            if half == 0:
                mine = self.wbuf.at[s, self.h, c, self.yh, pl.ds(0, 12)]
            else:
                mine = self.wbuf.at[s, :, c, :, self.unit(1, x)]
            for d in (2, 1, 3):
                to = at_chip(x, y + d, z, c) if half == 0 else at_chip(x + d, y, z, c)
                self.launch(self.remote(mine, mine, sm["p2s"].at[s, half, d - 1], sm["p2r"].at[s, half, d - 1], to))

    def third(self, s):
        sm, x, y, z, c = self.sems, self.x, self.y, self.z, self.c
        for half in range(2):
            for d in (1, 3, 2):
                if half == 0:
                    hh, yy = self.split(lax.rem(y + 4 - d, 4))
                    there = self.wbuf.at[s, hh, c, yy, pl.ds(0, 12)]
                else:
                    there = self.wbuf.at[s, :, c, :, self.unit(1, lax.rem(x + 4 - d, 4))]
                self.remote(there, there, sm["p2s"].at[s, half, d - 1], sm["p2r"].at[s, half, d - 1], (self.b, self.g)).wait_recv()
        mine = self.wbuf.at[s, :, c]
        self.launch(self.remote(mine, mine, sm["cs"].at[s], sm["cr"].at[s], at_chip(x, y, z, 1 - c)))

    def ready(self, s):
        there = self.wbuf.at[s, :, 1 - self.c]
        self.remote(there, there, self.sems["cs"].at[s], self.sems["cr"].at[s], (self.b, self.g)).wait_recv()

    def finish(self):
        self.drain_scatter()
        for cp, cond in self.pending:
            if cond is None:
                cp.wait_send()
            else:
                pl.when(cond)(lambda cp=cp: cp.wait_send())


def exchange_sems():
    D = pltpu.SemaphoreType.DMA
    return {"scat": D((2, 4, 2)), "own": D((3, 2)), "zs": D((3, 5, 2)), "p1s": D((3, 2, 3)), "p1r": D((3, 2, 3)),
            "p2s": D((3, 2, 3)), "p2r": D((3, 2, 3)), "cs": D((3,)), "cr": D((3,)), "os": D((13,)), "or": D((13,)), "oloc": D((2,))}


def exchange_kernel(tree, screen, orb, wbuf, rows, subs, *flat):
    ex = Exchange(screen, orb, wbuf, rows, subs, jax.tree.unflatten(tree, flat))
    ex.barrier()
    ex.scatter()
    ex.orbitals_out()
    ex.first(1)
    ex.first(2)
    ex.second(1)
    ex.first(0)
    ex.second(2)
    ex.orbitals_on()
    ex.third(1)
    ex.second(0)
    ex.third(2)
    ex.third(0)
    ex.orbitals_done()
    for s in range(3):
        ex.ready(s)
    ex.finish()


def compute_kernel(tree, slot_ref, rows_ref, subs_ref, w_ref, lower, upper, *flat):
    sc = jax.tree.unflatten(tree, flat)
    g6 = lax.axis_index("grp") * 6
    rep, tile = select_matrix(False), select_matrix(True)
    for r in range(3):
        expand_rows(rows_ref[r], sc["urep"][r], sc["stage"], rep)
        valence(sc["stage"], sc["uv"][r])
        expand_cols(subs_ref[r], sc["utile"][r], sc["pt"][r], tile)
    for s in (1, 2, 0):
        jobs = [(sc["urep"][0], sc["utile"][s], sc["yr"][0], sc["yi"][0])]
        if s:
            jobs.append((sc["urep"][s], sc["utile"][0], sc["yr"][1], sc["yi"][1]))

        def load_w(slot):
            part = slot // 3
            w = w_ref[s, part // 4, part // 2 % 2, part % 2, pl.ds(slot % 3 * 8, 8)]
            return w[0:4].reshape(128, 128), w[4:8].reshape(128, 128)
        mix(load_w, slot_ref, s, g6, jobs)
        close(sc["yr"][0], sc["yi"][0], sc["uv"][0], sc["pt"][s], sc["acc"], sc["tr"], sc["ti"])
        emit_lower(sc["tr"], sc["ti"], lower, s)
        if s:
            close(sc["yr"][1], sc["yi"][1], sc["uv"][s], sc["pt"][0], sc["acc"], sc["tr"], sc["ti"])
            emit_upper(sc["tr"], sc["ti"], upper, s - 1)


def body(orbitals, screen, slot_of_q):
    vmem = pl.BlockSpec(memory_space=pltpu.VMEM)
    leaves, tree = jax.tree.flatten(exchange_sems())
    w, rows, subs = pl.pallas_call(
        functools.partial(exchange_kernel, tree),
        out_shape=[
            jax.ShapeDtypeStruct((3, 2, 2, 2, 24, 32, 128), BF),
            jax.ShapeDtypeStruct((3, 24, 2, 8, 128), BF),
            jax.ShapeDtypeStruct((3, 6, 2, 8, 128), BF),
        ],
        in_specs=[vmem] * 2,
        out_specs=[vmem] * 3,
        scratch_shapes=leaves,
        compiler_params=pltpu.CompilerParams(collective_id=0, has_side_effects=True, vmem_limit_bytes=40 << 20),
        name="exchange",
    )(screen.reshape(2, 24, 32, 128), orbitals)
    leaves, tree = jax.tree.flatten(scratch())
    return pl.pallas_call(
        functools.partial(compute_kernel, tree),
        out_shape=[
            jax.ShapeDtypeStruct((1, 3, 2, 384, 96), BF),
            jax.ShapeDtypeStruct((1, 2, 2, 96, 384), BF),
        ],
        in_specs=[pl.BlockSpec(memory_space=pltpu.SMEM)] + [vmem] * 3,
        out_specs=[vmem] * 2,
        scratch_shapes=leaves,
        compiler_params=pltpu.CompilerParams(vmem_limit_bytes=48 << 20),
        name="pairs",
    )(slot_of_q, rows, subs, w)


def solution(mesh):
    in_specs = (P(("blk", "grp"), None, None, None), P("blk", "grp", None, None, None), P())
    out_specs = (P("blk", None, None, None, "grp"), P("blk", None, None, "grp", None))
    return jax.shard_map(body, mesh=mesh, in_specs=in_specs, out_specs=out_specs, check_vma=False)
```

time: 1500 us -> 72.1 us (0.05)
  waiting for transfers between devices: 1310 us -> 0 us
  Pallas kernels: 0 us -> 67.3 us
  blocking collectives: 64.4 us -> 0 us
  local copies, waits for them, and re-layouts: 57.1 us -> 3.4 us
  matrix products: 18 us -> 0 us
  starting transfers between devices: 17.8 us -> 0 us
  other arithmetic: 16.4 us -> 0 us
    psum x1 -> x0, waiting for transfers between devices: 1240 us -> none  [spread(): return lax.psum(jnp.where(mine, array, jnp.zeros_like(array)), axis)]
    pallas_call x0 -> x2, Pallas kernels: none -> 67.3 us  [the longest x1 52.6 us: body(): pl.pallas_call(functools.partial(exchange_kernel, tree), out_shape=[jax.S...]
    all_gather x1 -> x0, blocking collectives: 64.4 us -> none  [body(): left_rows = lax.all_gather(orbitals, 'grp', axis=0, tiled=True)]
    all_gather x3 -> x0, waiting for transfers between devices: 59.9 us -> none  [body(): screen_row = lax.all_gather(screen_piece, 'grp', axis=0, tiled=True)]
    gather x11 -> x0, local copies, waits for them, and re-layouts: 22.5 us -> none  [the longest x7 12.8 us: take_rows(): return jnp.take(block, order, axis=1)]
    dot_general x24 -> x0, matrix products: 18 us -> none  [the longest x12 11.6 us: close_pairs(): jnp.einsum('gqan,gqbn->gqab', left, right, preferred_element_type=jnp.flo...]
    ppermute x4 -> x0, starting transfers between devices: 17.6 us -> none  [shifted(): return lax.ppermute(value, axis, pairs)]
  transfers between devices with their start and end apart: 8 -> 0, of which waited for: 4 -> 0; matrix products, arithmetic and copies ran while one was open for 2% -> 0% of each run, Pallas kernels for 0% -> 0%
where the time goes in v1:
time: 72.1 us; the launch traced here: 71.3 us
  Pallas kernels  67.3 us (93%)
  local copies, waits for them, and re-layouts  3.4 us (5%)
    pallas_call x1, Pallas kernels, body(): pl.pallas_call(functools.partial(exchange_kernel, tree), out_shape=[jax.S...  52.6 us
    pallas_call x1, Pallas kernels, body(): pl.pallas_call(functools.partial(compute_kernel, tree), out_shape=[jax.Sh...  14.6 us
    unnamed x6, local copies, waits for them, and re-layouts  2.4 us

profile of v1, /device:TPU:1, one launch (start us, length us, event | category | flops | bytes accessed | tf_op | source)
XLA Modules:
  0.0 71.3 jit_solution(15125076464875975535)
XLA Ops:
  0.6 0.0 copy-start
  0.6 1.0 %copy-done = bf16[1,6,2,128,128]{4,3,2,1,0:T(8,128)(2,1)S(1)} copy-done((bf16[1,6,2,128,128]{4,3,2,1,0:T(8,128)(2,1)S(1)}, bf16[1,6,2,128,128]{4,3,2,1,0:T(8,128)(2,1)}, u32[]{:S(2)}) %copy-start) | copy-done | bytes 393240
  1.6 0.0 copy-start.1
  1.6 0.7 %copy-done.1 = bf16[6,2,8,128]{3,2,1,0:T(8,128)(2,1)S(1)} copy-done((bf16[6,2,8,128]{3,2,1,0:T(8,128)(2,1)S(1)}, bf16[6,2,8,128]{3,2,1,0:T(8,128)(2,1)}, u32[]{:S(2)}) %copy-start.1) | copy-done | bytes 24600
  2.4 52.6 %exchange.1 = (bf16[3,2,2,2,24,32,128]{6,5,4,3,2,1,0:T(8,128)(2,1)S(1)}, bf16[3,24,2,8,128]{4,3,2,1,0:T(8,128)(2,1)S(1)}, bf16[3,6,2,8,128]{4,3,2,1,0:T(8,128)(2,1)S(1)}) custom-call(bf16[2,24,32,128]{3,2,1,0:T(8,128)(2,1)S(1)} %bitcast.1, bf16[6,2,8,128]{3,2,1,0:T(8,128)(2,1)S(1)} %copy-done.1), custom_call_target="tpu_custom_call" | custom-call | tf_op jit(solution)/shard_map/exchange/pallas_call | solution.py:372
  55.0 0.0 copy-start.2
  55.0 0.7 copy-done.2
  55.7 14.6 %pairs.1 = (bf16[1,3,2,384,96]{4,3,2,1,0:T(8,128)(2,1)S(1)}, bf16[1,2,2,96,384]{4,3,2,1,0:T(8,128)(2,1)}) custom-call(s32[3,24]{1,0:T(4,128)S(1)} %copy-done.2, bf16[3,24,2,8,128]{4,3,2,1,0:T(8,128)(2,1)S(1)} %get-tuple-element.5.rows_ref, bf16[3,6,2,8,128]{4,3,2,1,0:T(8,128)(2,1)S(1)} %get-tuple-element.6.subs_ref, ...), custom_call_target="tpu_custom_call" | custom-call | tf_op jit(solution)/shard_map/pairs/pallas_call | solution.py:386
  70.3 1.0 %copy.5 = bf16[1,3,2,384,96]{3,4,2,1,0:T(8,128)(2,1)} copy(bf16[1,3,2,384,96]{4,3,2,1,0:T(8,128)(2,1)S(1)} %get-tuple-element.8) | data formatting | bytes 884736 | tf_op jit(solution)/shard_map/pairs/pallas_call | solution.py:386
Async XLA Ops:
  0.6 1.0 %copy-start = (bf16[1,6,2,128,128]{4,3,2,1,0:T(8,128)(2,1)S(1)}, bf16[1,6,2,128,128]{4,3,2,1,0:T(8,128)(2,1)}, u32[]{:S(2)}) copy-start(bf16[1,6,2,128,128]{4,3,2,1,0:T(8,128)(2,1)} %param.4) | copy-start | bytes 1179652
  1.6 0.7 %copy-start.1 = (bf16[6,2,8,128]{3,2,1,0:T(8,128)(2,1)S(1)}, bf16[6,2,8,128]{3,2,1,0:T(8,128)(2,1)}, u32[]{:S(2)}) copy-start(bf16[6,2,8,128]{3,2,1,0:T(8,128)(2,1)} %orb.1) | copy-start | bytes 73732
  55.0 0.7 copy-start.2

commit v2 on v1

v2 whole, which is shorter than its diff:
```python
import functools
import jax
import jax.numpy as jnp
from jax import lax
from jax.experimental import pallas as pl
from jax.experimental.pallas import tpu as pltpu
from jax.sharding import PartitionSpec as P

BF = jnp.bfloat16
F32 = jnp.float32


def select_matrix(tile):
    r = lax.broadcasted_iota(jnp.int32, (256, 128), 0)
    col = lax.broadcasted_iota(jnp.int32, (256, 128), 1)
    band = (r % 4) if tile else ((r // 4) % 4)
    return (col == (r // 16) * 8 + 4 + band).astype(F32).astype(BF)


def expand_rows(x, dst, stage, sel):
    x2 = x.reshape(384, 128)
    for i in range(3):
        dst[pl.ds(i * 256, 256), :] = jnp.dot(sel, x2[i * 128:(i + 1) * 128], preferred_element_type=F32)
    stage[...] = x2.astype(F32)


def valence(stage, dst):
    for p in range(2):
        for v in range(4):
            dst[p * 4 + v] = stage[pl.ds(p * 8 + v, 24, stride=16), :]


def expand_cols(x, dst, pt, sel):
    x2 = x.reshape(96, 128)
    dst[...] = jnp.dot(sel[:192, :96], x2, preferred_element_type=F32)
    n = lax.broadcasted_iota(jnp.int32, (8, 128), 0)
    l = lax.broadcasted_iota(jnp.int32, (8, 128), 1)
    g = (n == l % 4).astype(F32)
    dn = (((0,), (0,)), ((), ()))
    for j in range(6):
        a = lax.dot_general(x[j, 0].astype(F32), g, dn, preferred_element_type=F32).astype(BF)
        b = lax.dot_general(x[j, 1].astype(F32), g, dn, preferred_element_type=F32).astype(BF)
        pt[j, 0:128, 0:128] = a
        pt[j, 0:128, 128:256] = -b
        pt[j, 128:256, 0:128] = b
        pt[j, 128:256, 128:256] = a


def mix(load_w, slot_ref, s, g6, jobs):
    def step(q, carry):
        wr, wi = load_w(slot_ref[s, q])
        wc = jnp.concatenate([jnp.concatenate([wr, wi], 1), jnp.concatenate([-wi, wr], 1)], 0)
        rows = []
        for urep, utile, _, _ in jobs:
            for j in range(6):
                k = lax.rem(g6 + j + q, 24)
                at = pl.multiple_of(k * 32, 32)
                ar = urep[pl.ds(at, 16), :]
                ai = urep[pl.ds(at + 16, 16), :]
                br = utile[j * 32:j * 32 + 16, :]
                bi = utile[j * 32 + 16:j * 32 + 32, :]
                rows.append(jnp.concatenate([(ar * br + ai * bi).astype(BF), (ar * bi - ai * br).astype(BF)], 1))
        y = jnp.dot(jnp.concatenate(rows, 0), wc, preferred_element_type=F32)
        for n, (_, _, yr, yi) in enumerate(jobs):
            for j in range(6):
                k = lax.rem(g6 + j + q, 24)
                r0 = (n * 6 + j) * 16
                yr[pl.ds(j * 384 + k, 16, stride=24), :] = y[r0:r0 + 16, 0:128]
                yi[pl.ds(j * 384 + k, 16, stride=24), :] = y[r0:r0 + 16, 128:256]
        return carry
    lax.fori_loop(0, 24, step, 0, unroll=8)


def close(yr, yi, uv, pt, acc, tr, ti):
    lane = lax.broadcasted_iota(jnp.int32, (256, 256), 1) % 128 // 4

    def step(j, carry):
        ur = uv[0:4]
        ui = uv[4:8]
        p = pt[j]
        weights = jnp.concatenate([jnp.where(lane == j * 4 + c2, p, jnp.zeros_like(p)) for c2 in range(4)], 0)
        blocks = []
        for c in range(4):
            parts = []
            for c2 in range(4):
                at = pl.multiple_of(j * 384 + (c * 4 + c2) * 24, 8)
                a = yr[pl.ds(at, 24), :][None]
                b = yi[pl.ds(at, 24), :][None]
                parts.append((a * ur - b * ui).reshape(96, 128).astype(BF))
                parts.append((a * ui + b * ur).reshape(96, 128).astype(BF))
            blocks.append(jnp.concatenate(parts, 1))
        d = jnp.dot(jnp.concatenate(blocks, 0), weights, preferred_element_type=F32)

        acc[...] += d
        return carry
    acc[...] = jnp.zeros_like(acc)
    lax.fori_loop(0, 6, step, 0, unroll=6)
    for cv in range(16):
        tr[pl.ds(cv, 24, stride=16), :] = acc[cv * 24:cv * 24 + 24, 0:128]
        ti[pl.ds(cv, 24, stride=16), :] = acc[cv * 24:cv * 24 + 24, 128:256]


def emit_lower(tr, ti, out, s):
    out[0, s, 0] = tr[...].T[0:96, :].astype(BF)
    out[0, s, 1] = ti[...].T[0:96, :].astype(BF)


def emit_upper(tr, ti, out, t):
    out[0, t, 0] = tr[...].T[0:96, :].astype(BF)
    out[0, t, 1] = (-ti[...]).T[0:96, :].astype(BF)


def scratch():
    return dict(
        urep=[pltpu.VMEM((768, 128), F32)] * 3,
        uv=[pltpu.VMEM((8, 24, 128), F32)] * 3,
        utile=[pltpu.VMEM((192, 128), F32)] * 3,
        pt=[pltpu.VMEM((6, 256, 256), BF)] * 3,
        stage=pltpu.VMEM((384, 128), F32),
        yr=[pltpu.VMEM((2304, 128), F32)] * 2,
        yi=[pltpu.VMEM((2304, 128), F32)] * 2,
        acc=pltpu.VMEM((384, 256), F32),
        tr=pltpu.VMEM((384, 128), F32),
        ti=pltpu.VMEM((384, 128), F32),
    )


MESH = pl.DeviceIdType.MESH


def place():
    b = lax.axis_index("blk")
    g = lax.axis_index("grp")
    return (b // 16) % 4, (b // 64) * 2 + g // 2, b % 16, g % 2


def at_chip(x, y, z, c):
    x, y, z = lax.rem(x, 4), lax.rem(y, 4), lax.rem(z, 16)
    return (y // 2) * 64 + x * 16 + z, (y % 2) * 2 + c


class Exchange:
    def __init__(self, screen, orb, wbuf, rows, subs, sems):
        self.screen, self.orb, self.wbuf, self.rows, self.subs = screen, orb, wbuf, rows, subs
        self.sems = sems
        self.x, self.y, self.z, self.c = place()
        self.b, self.g = lax.axis_index("blk"), lax.axis_index("grp")
        self.h = jnp.where((self.y == 1) | (self.y == 2), 1, 0)
        self.yh = self.y // 2
        self.source = (self.x == 0) & (self.y < 2) & (self.z < 3)
        self.pending = []

    def row(self, off):
        return lax.rem(self.b + off + 128, 128)

    def signal(self, sem, to, cond=None):
        def go():
            pl.semaphore_signal(sem, inc=1, device_id=to, device_id_type=MESH)
        if cond is None:
            go()
        else:
            pl.when(cond)(go)

    def barrier(self):
        bar = pltpu.get_barrier_semaphore()
        x, y, z, c, g = self.x, self.y, self.z, self.c, self.g
        near = [at_chip(x + d, y, z, c) for d in (1, 2, 3)] + [at_chip(x, y + d, z, c) for d in (1, 2, 3)]
        near += [(self.b, lax.rem(g + d, 4)) for d in (1, 2, 3)]
        for d in near:
            self.signal(bar, d)

        @pl.when(self.source)
        def _():
            for xx in range(4):
                for yh in range(2):
                    if xx or yh:
                        self.signal(bar, self.target(xx, yh))
        self.signal(bar, at_chip(0, self.h, z, c), (z < 3) & jnp.logical_not(self.source))
        for k in (1, 2, 3):
            self.signal(bar, at_chip(x, y, z + k, c), z + k < 16)
        self.signal(bar, at_chip(x, y, 15, c), z == 0)
        self.signal(bar, (self.row(-1), g), z == 0)
        self.signal(bar, (self.row(-2), g), z < 2)
        count = len(near) + jnp.where(self.source, 7, jnp.where(z < 3, 1, 0))
        count += jnp.minimum(z, 3) + jnp.where(z == 15, 3, jnp.where(z == 14, 1, 0))
        pl.semaphore_wait(bar, count)
        for k in (1, 2, 3):
            self.signal(self.sems["rdyz"].at[k - 1], at_chip(x, y, z + 16 - k, c), z >= k)
        self.signal(self.sems["rdyw"], at_chip(x, y, 0, c), z == 15)
        self.signal(self.sems["rdyr"].at[0], (self.row(1), g), z == 15)
        self.signal(self.sems["rdyr"].at[1], (self.row(2), g), z >= 14)

    def await_up(self, s, only=None):
        z = self.z
        for k in (1, 2, 3):
            early = {1: ((z == 1) & (k < 3)) | ((z == 3) & (k != 2)) | (z == 6) | ((z == 12) & (k == 1)),
                     2: (z == 2) & (k == 1), 0: z == 0}
            if s is None:
                cond = (z + k < 16) & jnp.logical_not(early[0] | early[1] | early[2])
            else:
                cond = early[s] if only is None else early[s] & only
            pl.when(cond)(lambda k=k: pl.semaphore_wait(self.sems["rdyz"].at[k - 1], 1))

    def target(self, xx, yh):
        return at_chip(xx, self.y if yh == 0 else 3 - self.y, self.z, self.c)

    def remote(self, src, dst, send, recv, to):
        return pltpu.make_async_remote_copy(src_ref=src, dst_ref=dst, send_sem=send, recv_sem=recv, device_id=to, device_id_type=MESH)

    def launch(self, cp, cond=None):
        if cond is None:
            cp.start()
        else:
            pl.when(cond)(lambda: cp.start())
        self.pending.append((cp, cond))

    def unit(self, half, x):
        return pl.ds(half * 12 + x * 3, 3)

    def own(self, s, half):
        return self.wbuf[s].at[self.h, self.c, self.yh, self.unit(half, self.x)]

    def scattered(self, s):
        sm = self.sems
        for half in range(2):
            for xx, yh in ((2, 1), (1, 1), (3, 1), (2, 0), (1, 0), (3, 0), (0, 1)):
                yield self.remote(self.screen.at[yh, self.unit(half, xx)], self.wbuf[s].at[self.h, self.c, yh, self.unit(half, xx)],
                                  sm["scat"].at[half, xx, yh], sm["own"].at[s, half], self.target(xx, yh))

    def scatter(self):
        for s in range(3):
            @pl.when(self.source & (self.z == s))
            def _():
                for cp in self.scattered(s):
                    cp.start()
                for half in range(2):
                    pltpu.make_async_copy(self.screen.at[0, self.unit(half, 0)], self.wbuf[s].at[self.h, self.c, 0, self.unit(half, 0)],
                                          self.sems["own"].at[s, half]).start()

    def drain_scatter(self):
        for s in range(3):
            @pl.when(self.source & (self.z == s))
            def _():
                for cp in self.scattered(s):
                    cp.wait_send()

    def orbitals_out(self):
        sm, g = self.sems, self.g
        self.o_in = []
        self.o_local = [pltpu.make_async_copy(self.orb, self.rows.at[0, pl.ds(g * 6, 6)], sm["oloc"].at[0]),
                        pltpu.make_async_copy(self.orb, self.subs.at[0], sm["oloc"].at[1])]
        for cp in self.o_local:
            cp.start()
        self.o_row = []
        for n, (off, dst) in enumerate(((-1, self.rows.at[1, pl.ds(g * 6, 6)]), (-2, self.rows.at[2, pl.ds(g * 6, 6)]),
                                        (1, self.subs.at[1]), (2, self.subs.at[2]))):
            self.o_row.append(self.remote(self.orb, dst, sm["os"].at[n], sm["or"].at[n], (self.row(off), g)))
        self.group_out(0, self.orb, 4)
        z = self.z
        self.launch(self.o_row[0], z >= 1)
        self.launch(self.o_row[1], z >= 2)
        self.launch(self.o_row[2], z == 15)
        self.launch(self.o_row[3], z >= 14)

    def orbitals_up(self):
        self.launch(self.o_row[2], self.z < 15)
        self.launch(self.o_row[3], self.z < 14)

    def orbitals_wrap(self):
        z = self.z
        pl.when(z == 0)(lambda: pl.semaphore_wait(self.sems["rdyr"].at[0], 1))
        pl.when(z < 2)(lambda: pl.semaphore_wait(self.sems["rdyr"].at[1], 1))
        self.launch(self.o_row[0], z == 0)
        self.launch(self.o_row[1], z < 2)

    def group_out(self, r, src, base):
        for d in (1, 2, 3):
            n = base + d - 1
            cp = self.remote(src, self.rows.at[r, pl.ds(self.g * 6, 6)], self.sems["os"].at[n], self.sems["or"].at[n],
                             (self.b, lax.rem(self.g + d, 4)))
            self.launch(cp)
            back = lax.rem(self.g + 4 - d, 4)
            self.o_in.append(self.remote(src, self.rows.at[r, pl.ds(back * 6, 6)], self.sems["os"].at[n], self.sems["or"].at[n],
                                         (self.b, lax.rem(self.g + d, 4))))

    def orbitals_on(self):
        for r in (1, 2):
            self.o_row[r - 1].wait_recv()
            self.group_out(r, self.rows.at[r, pl.ds(self.g * 6, 6)], 4 + 3 * r)

    def orbitals_done(self):
        for cp in self.o_local:
            cp.wait()
        for cp in self.o_row[2:] + self.o_in:
            cp.wait_recv()

    def first(self, s, only=None):
        sm, x, y, z, c = self.sems, self.x, self.y, self.z, self.c
        hops = ((3, (z == 3) | (z == 6) | (z == (0 if s == 0 else 3))), (2, (z == 6) | (z == (s if s < 2 else 6))),
                (15, (z == 6) | (z == 15) | (z == 12) | (z == (s if s else 6))), (13, z == 15),
                (1, (z == 3) | (z == 6) | (z == 12) | (z == s)), (14, (z == 12) | (z == (2 if s == 2 else 12))))
        for half in range(2):
            mine = self.own(s, half)
            cp = self.remote(mine, mine, sm["zs"].at[s, 0, half], sm["own"].at[s, half], (self.b, self.g))
            if only is None:
                cp.wait_recv()
            else:
                pl.when(only)(cp.wait_recv)
            if half == 0:
                self.await_up(s, only)
            for n, (off, cond) in enumerate(hops):
                cond = cond if only is None else cond & only
                self.launch(self.remote(mine, mine, sm["zs"].at[s, n, half], sm["own"].at[s, half], at_chip(x, y, z + off, c)), cond)
            for d in (2, 1, 3):
                to = at_chip(x + d, y, z, c) if half == 0 else at_chip(x, y + d, z, c)
                self.launch(self.remote(mine, mine, sm["p1s"].at[s, half, d - 1], sm["p1r"].at[s, half, d - 1], to), only)

    def down(self, s):
        sm, z = self.sems, self.z
        if s == 1:
            pl.when(z == 0)(lambda: pl.semaphore_wait(sm["rdyw"], 1))
        for half in range(2):
            mine = self.own(s, half)
            self.launch(self.remote(mine, mine, sm["ds"].at[s, half], sm["own"].at[s, half], at_chip(self.x, self.y, 15, self.c)), z == 0)

    def split(self, y):
        return jnp.where((y == 1) | (y == 2), 1, 0), y // 2

    def part(self, s, half, d, c):
        if half == 0:
            hh, yy = self.split(lax.rem(self.y + 4 - d, 4))
            return self.wbuf[s].at[hh, c, yy, pl.ds(0, 12)]
        return self.wbuf[s].at[:, c, :, self.unit(1, lax.rem(self.x + 4 - d, 4))]

    def to_sibling(self, s, half, d):
        mine = self.part(s, half, d, self.c)
        self.launch(self.remote(mine, mine, self.sems["cs"].at[s, half, d], self.sems["cr"].at[s, half, d],
                                at_chip(self.x, self.y, self.z, 1 - self.c)))

    def second(self, s):
        sm, x, y, z, c = self.sems, self.x, self.y, self.z, self.c
        for half in range(2):
            for d in (1, 3, 2):
                if half == 0:
                    there = self.wbuf[s].at[self.h, c, self.yh, self.unit(0, lax.rem(x + 4 - d, 4))]
                else:
                    hh, yy = self.split(lax.rem(y + 4 - d, 4))
                    there = self.wbuf[s].at[hh, c, yy, self.unit(1, x)]
                self.remote(there, there, sm["p1s"].at[s, half, d - 1], sm["p1r"].at[s, half, d - 1], (self.b, self.g)).wait_recv()
            mine = self.part(s, half, 0, c)
            for d in (2, 1, 3):
                to = at_chip(x, y + d, z, c) if half == 0 else at_chip(x + d, y, z, c)
                self.launch(self.remote(mine, mine, sm["p2s"].at[s, half, d - 1], sm["p2r"].at[s, half, d - 1], to))
            self.to_sibling(s, half, 0)

    def third(self, s, steps):
        sm = self.sems
        for d in steps:
            for half in range(2):
                there = self.part(s, half, d, self.c)
                self.remote(there, there, sm["p2s"].at[s, half, d - 1], sm["p2r"].at[s, half, d - 1], (self.b, self.g)).wait_recv()
                self.to_sibling(s, half, d)

    def ready(self, s):
        for d in (0, 1, 3, 2):
            for half in range(2):
                there = self.part(s, half, d, 1 - self.c)
                self.remote(there, there, self.sems["cs"].at[s, half, d], self.sems["cr"].at[s, half, d], (self.b, self.g)).wait_recv()

    def finish(self):
        self.drain_scatter()
        for cp, cond in self.pending:
            if cond is None:
                cp.wait_send()
            else:
                pl.when(cond)(lambda cp=cp: cp.wait_send())


def exchange_sems():
    D = pltpu.SemaphoreType.DMA
    return {"scat": D((2, 4, 2)), "own": D((3, 2)), "zs": D((3, 6, 2)), "p1s": D((3, 2, 3)), "p1r": D((3, 2, 3)),
            "p2s": D((3, 2, 3)), "p2r": D((3, 2, 3)), "cs": D((3, 2, 4)), "cr": D((3, 2, 4)), "ds": D((3, 2)), "os": D((13,)), "or": D((13,)), "oloc": D((2,)),
            "rdyz": pltpu.SemaphoreType.REGULAR((3,)), "rdyw": pltpu.SemaphoreType.REGULAR, "rdyr": pltpu.SemaphoreType.REGULAR((2,))}


def buffers():
    return {"w": [pltpu.VMEM((2, 2, 2, 24, 32, 128), BF)] * 3, "rows": pltpu.VMEM((3, 24, 2, 8, 128), BF), "subs": pltpu.VMEM((3, 6, 2, 8, 128), BF),
            "slot": pltpu.SMEM((3, 24), jnp.int32), "slot_sem": pltpu.SemaphoreType.DMA}


def kernel(tree, slot_ref, screen, orb, lower, upper, *flat):
    sc, buf, sems = jax.tree.unflatten(tree, flat)
    w_ref, slot_sm = buf["w"], buf["slot"]
    g6 = lax.axis_index("grp") * 6
    ex = Exchange(screen, orb, w_ref, buf["rows"], buf["subs"], sems)

    def prepare():
        rep, tile = select_matrix(False), select_matrix(True)
        for r in range(3):
            expand_rows(buf["rows"][r], sc["urep"][r], sc["stage"], rep)
            valence(sc["stage"], sc["uv"][r])
            expand_cols(buf["subs"][r], sc["utile"][r], sc["pt"][r], tile)

    def jobs_of(s):
        jobs = [(sc["urep"][0], sc["utile"][s], sc["yr"][0], sc["yi"][0])]
        if s:
            jobs.append((sc["urep"][s], sc["utile"][0], sc["yr"][1], sc["yi"][1]))
        return jobs

    def mixed(s):
        def load_w(slot):
            part = slot // 3
            w = w_ref[s][part // 4, part // 2 % 2, part % 2, pl.ds(slot % 3 * 8, 8)]
            return w[0:4].reshape(128, 128), w[4:8].reshape(128, 128)
        mix(load_w, slot_sm, s, g6, jobs_of(s))

    def low(s):
        close(sc["yr"][0], sc["yi"][0], sc["uv"][0], sc["pt"][s], sc["acc"], sc["tr"], sc["ti"])
        emit_lower(sc["tr"], sc["ti"], lower, s)

    def high(s):
        close(sc["yr"][1], sc["yi"][1], sc["uv"][s], sc["pt"][0], sc["acc"], sc["tr"], sc["ti"])
        emit_upper(sc["tr"], sc["ti"], upper, s - 1)

    slots = pltpu.make_async_copy(slot_ref, slot_sm, buf["slot_sem"])
    slots.start()
    ex.barrier()
    ex.scatter()
    ex.orbitals_out()
    ex.first(1)
    ex.first(2)
    ex.first(0, ex.z == 0)
    ex.down(1)
    ex.down(2)
    ex.down(0)
    ex.second(1)
    ex.first(0, ex.z > 0)
    ex.await_up(None)
    ex.orbitals_up()
    ex.second(2)
    ex.orbitals_wrap()
    ex.orbitals_on()
    ex.third(1, (1, 3, 2))
    ex.second(0)
    ex.orbitals_done()
    prepare()
    slots.wait()
    ex.ready(1)
    mixed(1)
    ex.third(2, (1, 3, 2))
    low(1)
    high(1)
    ex.third(0, (1, 3, 2))
    ex.ready(2)
    mixed(2)
    low(2)
    high(2)
    ex.ready(0)
    mixed(0)
    low(0)
    ex.finish()


def body(orbitals, screen, slot_of_q):
    vmem = pl.BlockSpec(memory_space=pltpu.VMEM)
    leaves, tree = jax.tree.flatten((scratch(), buffers(), exchange_sems()))
    lower, upper = pl.pallas_call(
        functools.partial(kernel, tree),
        out_shape=[
            jax.ShapeDtypeStruct((1, 3, 2, 96, 384), BF),
            jax.ShapeDtypeStruct((1, 2, 2, 96, 384), BF),
        ],
        in_specs=[pl.BlockSpec(memory_space=pltpu.HBM)] * 3,
        out_specs=[vmem] * 2,
        scratch_shapes=leaves,
        compiler_params=pltpu.CompilerParams(collective_id=0, has_side_effects=True, vmem_limit_bytes=56 << 20),
        name="pairs",
    )(slot_of_q, screen.reshape(2, 24, 32, 128), orbitals)
    return jnp.swapaxes(lower, 3, 4), upper


def solution(mesh):
    in_specs = (P(("blk", "grp"), None, None, None), P("blk", "grp", None, None, None), P())
    out_specs = (P("blk", None, None, None, "grp"), P("blk", None, None, "grp", None))
    return jax.shard_map(body, mesh=mesh, in_specs=in_specs, out_specs=out_specs, check_vma=False)
```

time: 72.1 us -> 58.4 us (0.81)
  the two profiles are of different devices: /device:TPU:1 before, /device:TPU:337 now
where the time goes in v2:
time: 58.4 us; the launch traced here: 58.2 us
  Pallas kernels  55 us (94%)
  local copies, waits for them, and re-layouts  2.58 us (4%)
  between operations  0.65 us (1%)
    pallas_call x1, Pallas kernels, body(): pl.pallas_call(functools.partial(kernel, tree), out_shape=[jax.ShapeDtype...  55 us
    unnamed x4, local copies, waits for them, and re-layouts  2.58 us

profile of v2, /device:TPU:337, one launch (start us, length us, event | category | flops | bytes accessed | tf_op | source)
XLA Modules:
  0.0 58.2 jit_solution(3260374661220532441)
XLA Ops:
  0.6 55.0 %pairs.1 = (bf16[1,3,2,96,384]{4,3,2,1,0:T(8,128)(2,1)}, bf16[1,2,2,96,384]{4,3,2,1,0:T(8,128)(2,1)}) custom-call(s32[3,24]{1,0:T(4,128)} %slot_ref.1, bf16[2,24,32,128]{3,2,1,0:T(8,128)(2,1)} %bitcast.3, bf16[6,2,8,128]{3,2,1,0:T(8,128)(2,1)} %orb.1), custom_call_target="tpu_custom_call" | custom-call | tf_op jit(solution)/shard_map/pairs/pallas_call | solution.py:467
  55.6 0.0 copy-start
  55.6 1.9 %copy.7 = bf16[1,3,2,384,96]{3,4,2,1,0:T(8,128)(2,1)} copy(bf16[1,3,2,384,96]{3,4,2,1,0:T(8,128)(2,1)} %bitcast.2) | data formatting | bytes 884736
  57.5 0.0 copy-done
  57.5 0.7 %copy.8 = bf16[1,2,2,96,384]{4,3,2,1,0:T(8,128)(2,1)} copy(bf16[1,2,2,96,384]{4,3,2,1,0:T(8,128)(2,1)S(1)} %copy-done) | data formatting | bytes 589824
Async XLA Ops:
  55.6 1.9 %copy-start = (bf16[1,2,2,96,384]{4,3,2,1,0:T(8,128)(2,1)S(1)}, bf16[1,2,2,96,384]{4,3,2,1,0:T(8,128)(2,1)}, u32[]{:S(2)}) copy-start(bf16[1,2,2,96,384]{4,3,2,1,0:T(8,128)(2,1)} %get-tuple-element.9) | copy-start | bytes 884740

commit v3 on v2

--- a/solution.py
+++ b/solution.py
@@ -165,7 +165,7 @@
         bar = pltpu.get_barrier_semaphore()
         x, y, z, c, g = self.x, self.y, self.z, self.c, self.g
         near = [at_chip(x + d, y, z, c) for d in (1, 2, 3)] + [at_chip(x, y + d, z, c) for d in (1, 2, 3)]
-        near += [(self.b, lax.rem(g + d, 4)) for d in (1, 2, 3)]
+        near += [(self.b, lax.rem(g + d, 4)) for d in (1, 3)]
         for d in near:
             self.signal(bar, d)
 
@@ -193,7 +193,7 @@
     def await_up(self, s, only=None):
         z = self.z
         for k in (1, 2, 3):
-            early = {1: ((z == 1) & (k < 3)) | ((z == 3) & (k != 2)) | (z == 6) | ((z == 12) & (k == 1)),
+            early = {1: ((z == 1) & (k < 3)) | ((z == 3) & (k != 2)) | (z == 6) | ((z == 9) & (k == 1)),
                      2: (z == 2) & (k == 1), 0: z == 0}
             if s is None:
                 cond = (z + k < 16) & jnp.logical_not(early[0] | early[1] | early[2])
@@ -288,17 +288,21 @@
             self.o_row[r - 1].wait_recv()
             self.group_out(r, self.rows.at[r, pl.ds(self.g * 6, 6)], 4 + 3 * r)
 
-    def orbitals_done(self):
+    def orbitals_near(self):
         for cp in self.o_local:
             cp.wait()
-        for cp in self.o_row[2:] + self.o_in:
+        for cp in self.o_row[2:] + self.o_in[:3]:
+            cp.wait_recv()
+
+    def orbitals_done(self):
+        for cp in self.o_in[3:]:
             cp.wait_recv()
 
     def first(self, s, only=None):
         sm, x, y, z, c = self.sems, self.x, self.y, self.z, self.c
         hops = ((3, (z == 3) | (z == 6) | (z == (0 if s == 0 else 3))), (2, (z == 6) | (z == (s if s < 2 else 6))),
                 (15, (z == 6) | (z == 15) | (z == 12) | (z == (s if s else 6))), (13, z == 15),
-                (1, (z == 3) | (z == 6) | (z == 12) | (z == s)), (14, (z == 12) | (z == (2 if s == 2 else 12))))
+                (14, (z == 15) | (z == (2 if s == 2 else 15))), (1, (z == 3) | (z == 6) | (z == 9) | (z == s)))
         for half in range(2):
             mine = self.own(s, half)
             cp = self.remote(mine, mine, sm["zs"].at[s, 0, half], sm["own"].at[s, half], (self.b, self.g))
@@ -394,12 +398,19 @@
     g6 = lax.axis_index("grp") * 6
     ex = Exchange(screen, orb, w_ref, buf["rows"], buf["subs"], sems)
 
+    def prepare_rows(r):
+        expand_rows(buf["rows"][r], sc["urep"][r], sc["stage"], select_matrix(False))
+        valence(sc["stage"], sc["uv"][r])
+
     def prepare():
-        rep, tile = select_matrix(False), select_matrix(True)
+        prepare_rows(0)
+        tile = select_matrix(True)
         for r in range(3):
-            expand_rows(buf["rows"][r], sc["urep"][r], sc["stage"], rep)
-            valence(sc["stage"], sc["uv"][r])
             expand_cols(buf["subs"][r], sc["utile"][r], sc["pt"][r], tile)
+
+    def near():
+        ex.orbitals_near()
+        prepare()
 
     def jobs_of(s):
         jobs = [(sc["urep"][0], sc["utile"][s], sc["yr"][0], sc["yi"][0])]
@@ -428,22 +439,25 @@
     ex.scatter()
     ex.orbitals_out()
     ex.first(1)
+    ex.down(1)
+    ex.await_up(None)
+    ex.orbitals_up()
     ex.first(2)
+    ex.down(2)
     ex.first(0, ex.z == 0)
-    ex.down(1)
-    ex.down(2)
     ex.down(0)
     ex.second(1)
+    pl.when(ex.z <= 9)(near)
     ex.first(0, ex.z > 0)
-    ex.await_up(None)
-    ex.orbitals_up()
     ex.second(2)
     ex.orbitals_wrap()
     ex.orbitals_on()
     ex.third(1, (1, 3, 2))
     ex.second(0)
+    pl.when(ex.z > 9)(near)
     ex.orbitals_done()
-    prepare()
+    prepare_rows(1)
+    prepare_rows(2)
     slots.wait()
     ex.ready(1)
     mixed(1)

time: 58.4 us -> 57.2 us (0.979)
  the two profiles are of different devices: /device:TPU:337 before, /device:TPU:323 now
where the time goes in v3:
time: 57.2 us; the launch traced here: 57 us
  Pallas kernels  53.8 us (94%)
  local copies, waits for them, and re-layouts  2.58 us (5%)
  between operations  0.65 us (1%)
    pallas_call x1, Pallas kernels, body(): pl.pallas_call(functools.partial(kernel, tree), out_shape=[jax.ShapeDtype...  53.8 us
    unnamed x4, local copies, waits for them, and re-layouts  2.58 us

profile of v3, /device:TPU:323, one launch (start us, length us, event | category | flops | bytes accessed | tf_op | source)
XLA Modules:
  0.0 57.0 jit_solution(92861466894672166)
XLA Ops:
  0.6 53.8 %pairs.1 = (bf16[1,3,2,96,384]{4,3,2,1,0:T(8,128)(2,1)}, bf16[1,2,2,96,384]{4,3,2,1,0:T(8,128)(2,1)}) custom-call(s32[3,24]{1,0:T(4,128)} %slot_ref.1, bf16[2,24,32,128]{3,2,1,0:T(8,128)(2,1)} %bitcast.3, bf16[6,2,8,128]{3,2,1,0:T(8,128)(2,1)} %orb.1), custom_call_target="tpu_custom_call" | custom-call | tf_op jit(solution)/shard_map/pairs/pallas_call | solution.py:481
  54.4 0.0 copy-start
  54.4 1.9 %copy.7 = bf16[1,3,2,384,96]{3,4,2,1,0:T(8,128)(2,1)} copy(bf16[1,3,2,384,96]{3,4,2,1,0:T(8,128)(2,1)} %bitcast.2) | data formatting | bytes 884736
  56.3 0.0 copy-done
  56.3 0.7 %copy.8 = bf16[1,2,2,96,384]{4,3,2,1,0:T(8,128)(2,1)} copy(bf16[1,2,2,96,384]{4,3,2,1,0:T(8,128)(2,1)S(1)} %copy-done) | data formatting | bytes 589824
Async XLA Ops:
  54.4 1.9 %copy-start = (bf16[1,2,2,96,384]{4,3,2,1,0:T(8,128)(2,1)S(1)}, bf16[1,2,2,96,384]{4,3,2,1,0:T(8,128)(2,1)}, u32[]{:S(2)}) copy-start(bf16[1,2,2,96,384]{4,3,2,1,0:T(8,128)(2,1)} %get-tuple-element.9) | copy-start | bytes 884740
